TPU v7x, 256 devices: a whole 4x4x8 slice. The times are simulated.
256 devices in a mesh: img: 16 (over z, x_lo), txt: 16 (over y, x_hi, core).
Axes of the slice: x: 4 (x_hi: 2, x_lo: 2; x = x_hi * 2 + x_lo), y: 4, z: 8, core: 2. Of those that a mesh axis runs over, the one named last changes fastest.
Arguments:
- image_hidden: bfloat16 [8192, 1152], P(('img', 'txt')), may hold values from -12 to 12
- image_acts: bfloat16 [8192, 4304], P('img', 'txt'), may hold values from -6 to 6
- image_proj: bfloat16 [4304, 1152], P('txt'), may hold values from -0.09375 to 0.09375
- text_hidden: bfloat16 [8192, 1152], P(('txt', 'img')), may hold values from -12 to 12
- text_acts: bfloat16 [8192, 4304], P('txt', 'img'), may hold values from -6 to 6
- text_proj: bfloat16 [4304, 1152], P('img'), may hold values from -0.09375 to 0.09375
- positives: int32 [8192], P('img'), may hold values from 0 to 8191, each once
- log_scale: float32 [1], replicated, may hold values from 1.6 to 2.7
- bias: float32 [1], replicated, may hold values from -7 to -5
Outputs:
- loss: float32 [1], replicated
- image_grad: bfloat16 [8192, 1152], P(('img', 'txt'))
- text_grad: bfloat16 [8192, 1152], P(('txt', 'img'))
- image_act_grad: bfloat16 [8192, 4304], P('img', 'txt')
- text_act_grad: bfloat16 [8192, 4304], P('txt', 'img')
- image_proj_grad: float32 [4304, 1152], P('txt', 'img')
- text_proj_grad: float32 [4304, 1152], P('img', 'txt')
Inputs may be any that keep to these rules, and one draw needn't show every extreme that they name: `positives`: every text index is the positive of exactly one image.
All inputs are finite; a program needn't handle non-finite values.
Results may differ from a plain program's by a relative error of at most 0.007.
Values may be sent and summed in bfloat16 or wider, within the bound.
No kernel may reach another device: no remote copies, remote signals or barrier semaphores. Data moves between devices by JAX's collectives and lax.ppermute only.
A program may use at most 64 MiB of HBM per device.

v0:
```python
import jax
import jax.numpy as jnp
from jax import lax
from jax.sharding import PartitionSpec as P


def normalize(embed):
    values = embed.astype(jnp.float32)
    inverse = lax.rsqrt(jnp.sum(values * values, axis=-1, keepdims=True) + 1e-06)
    return (values * inverse, inverse)


def norm_backward(embed, upstream):
    unit, inverse = normalize(embed)
    return inverse * (upstream - unit * jnp.sum(unit * upstream, axis=-1, keepdims=True))


def contract_rows(left, right):
    return lax.dot_general(
        left, right, (((0,), (0,)), ((), ())), preferred_element_type=jnp.float32
    )


def contract_cols(left, right):
    return lax.dot_general(
        left, right, (((1,), (1,)), ((), ())), preferred_element_type=jnp.float32
    )


def on_device(
    image_hidden,
    image_acts,
    image_proj,
    text_hidden,
    text_acts,
    text_proj,
    positives,
    log_scale,
    bias,
):
    rows = image_hidden.shape[0]
    total_rows = rows * lax.axis_size("img") * lax.axis_size("txt")
    image_sum = lax.psum_scatter(
        jnp.dot(image_acts, image_proj, preferred_element_type=jnp.float32),
        "txt",
        scatter_dimension=0,
        tiled=True,
    )
    text_sum = lax.psum_scatter(
        jnp.dot(text_acts, text_proj, preferred_element_type=jnp.float32),
        "img",
        scatter_dimension=0,
        tiled=True,
    )
    image_embed = (image_hidden.astype(jnp.float32) + image_sum).astype(jnp.bfloat16)
    text_embed = (text_hidden.astype(jnp.float32) + text_sum).astype(jnp.bfloat16)
    image_block = lax.all_gather(image_embed, "txt", axis=0, tiled=True)
    text_block = lax.all_gather(text_embed, "img", axis=0, tiled=True)
    image_unit = normalize(image_block)[0].astype(jnp.bfloat16)
    text_unit = normalize(text_block)[0].astype(jnp.bfloat16)
    scale = jnp.exp(log_scale[0])
    text_count = text_block.shape[0]
    scores = scale * contract_cols(image_unit, text_unit) + bias[0]
    columns = lax.axis_index("txt") * text_count + lax.broadcasted_iota(
        jnp.int32, (1, text_count), 1
    )
    target = (positives[:, None] == columns).astype(jnp.float32)
    partial_loss = jnp.sum(jax.nn.softplus((1.0 - 2.0 * target) * scores))
    slope = (jax.nn.sigmoid(scores) - target).astype(jnp.bfloat16)
    image_dir = scale * jnp.dot(slope, text_unit, preferred_element_type=jnp.float32)
    text_dir = scale * contract_rows(slope, image_unit)
    total = lax.psum(partial_loss, ("img", "txt"))
    loss = jnp.reshape(total / total_rows, (1,))
    image_up = lax.psum_scatter(image_dir, "txt", scatter_dimension=0, tiled=True)
    text_up = lax.psum_scatter(text_dir, "img", scatter_dimension=0, tiled=True)
    image_grad = norm_backward(image_embed, image_up).astype(jnp.bfloat16)
    text_grad = norm_backward(text_embed, text_up).astype(jnp.bfloat16)
    image_back = lax.all_gather(image_grad, "txt", axis=0, tiled=True)
    text_back = lax.all_gather(text_grad, "img", axis=0, tiled=True)
    image_act_grad = contract_cols(image_back, image_proj).astype(jnp.bfloat16)
    text_act_grad = contract_cols(text_back, text_proj).astype(jnp.bfloat16)
    image_proj_grad = lax.psum_scatter(
        contract_rows(image_acts, image_back), "img", scatter_dimension=1, tiled=True
    )
    text_proj_grad = lax.psum_scatter(
        contract_rows(text_acts, text_back), "txt", scatter_dimension=1, tiled=True
    )
    return (
        loss,
        image_grad,
        text_grad,
        image_act_grad,
        text_act_grad,
        image_proj_grad,
        text_proj_grad,
    )


def solution(mesh):
    return jax.shard_map(
        on_device,
        mesh=mesh,
        in_specs=(
            P(("img", "txt"), None),
            P("img", "txt"),
            P("txt", None),
            P(("txt", "img"), None),
            P("txt", "img"),
            P("img", None),
            P("img"),
            P(),
            P(),
        ),
        out_specs=(
            P(),
            P(("img", "txt"), None),
            P(("txt", "img"), None),
            P("img", "txt"),
            P("txt", "img"),
            P("txt", "img"),
            P("img", "txt"),
        ),
        check_vma=False,
    )
```

profile of v0, /device:TPU:1, one launch (start us, length us, event | category | flops | bytes accessed | tf_op | source)
XLA Modules:
  0.0 891.1 jit_solution(4390650750124508196)
XLA Ops:
  7.2 0.0 reduce-scatter.7.cloned.1.call-start
  7.2 1.0 copy-done
  8.2 3.2 fusion.30
  11.5 0.0 reduce-scatter.9.cloned.1.call-start
  11.5 0.9 copy-done.8
  12.4 0.2 copy-done.9
  12.6 2.3 fusion.31
  14.9 0.0 all-gather.5.cloned.1.call-start
  15.0 79.3 %reduce-scatter.7.cloned.1.call-done = f32[32,1152]{1,0:T(8,128)} async-done(((f32[512,1152]{1,0:T(8,128)}), f32[32,1152]{1,0:T(8,128)}) %reduce-scatter.7.cloned.1.call-update) | async-done | bytes 147472 | tf_op jit(solution)/shard_map/reduce_scatter | solution.py:43
  94.3 1.7 fusion.26
  96.0 0.0 all-gather.7.cloned.1.call-start
  96.0 67.0 %reduce-scatter.9.cloned.1.call-done = f32[32,1152]{1,0:T(8,128)} async-done(((f32[512,1152]{1,0:T(8,128)}), f32[32,1152]{1,0:T(8,128)}) %reduce-scatter.9.cloned.1.call-update) | async-done | bytes 147472 | tf_op jit(solution)/shard_map/reduce_scatter | solution.py:49
  163.0 1.7 fusion.27
  164.7 0.0 reduce-scatter.11.cloned.1.call-start
  166.1 61.9 %all-gather.5.cloned.1.call-done = bf16[512,1152]{1,0:T(8,128)(2,1)} async-done(((bf16[32,1152]{1,0:T(8,128)(2,1)}), bf16[512,1152]{1,0:T(8,128)(2,1)}) %all-gather.5.cloned.1.call-update) | async-done | bytes 1179664 | tf_op jit(solution)/shard_map/all_gather | solution.py:57
  228.0 1.7 fusion
  229.7 58.4 %all-gather.7.cloned.1.call-done = bf16[512,1152]{1,0:T(8,128)(2,1)} async-done(((bf16[32,1152]{1,0:T(8,128)(2,1)}), bf16[512,1152]{1,0:T(8,128)(2,1)}) %all-gather.7.cloned.1.call-update) | async-done | bytes 1179664 | tf_op jit(solution)/shard_map/all_gather | solution.py:58
  288.0 1.6 fusion.2
  289.7 3.6 fusion.9
  293.3 2.5 convolution_multiply_fusion.1
  295.9 0.0 reduce-scatter.13.cloned.1.call-start
  295.9 2.4 convolution_multiply_fusion
  298.4 0.0 all-gather.9.cloned.1.call-start
  298.4 86.3 %reduce-scatter.11.cloned.1.call-done = f32[32,1152]{1,0:T(8,128)} async-done(((f32[512,1152]{1,0:T(8,128)}), f32[32,1152]{1,0:T(8,128)}) %reduce-scatter.11.cloned.1.call-update) | async-done | bytes 147472 | tf_op jit(solution)/shard_map/reduce_scatter | solution.py:74
  384.8 1.1 fusion.22
  385.9 1.6 fusion.25
  387.6 0.0 all-gather.11.cloned.1.call-start
  387.6 65.5 %reduce-scatter.13.cloned.1.call-done = f32[32,1152]{1,0:T(8,128)} async-done(((f32[512,1152]{1,0:T(8,128)}), f32[32,1152]{1,0:T(8,128)}) %reduce-scatter.13.cloned.1.call-update) | async-done | bytes 147472 | tf_op jit(solution)/shard_map/reduce_scatter | solution.py:75
  453.1 1.1 fusion.18
  454.2 1.6 fusion.21
  455.9 0.0 all-reduce.5.cloned.1.call-start
  455.9 62.0 %all-gather.9.cloned.1.call-done = bf16[512,1152]{1,0:T(8,128)(2,1)} async-done(((bf16[32,1152]{1,0:T(8,128)(2,1)}), bf16[512,1152]{1,0:T(8,128)(2,1)}) %all-gather.9.cloned.1.call-update) | async-done | bytes 1179664 | tf_op jit(solution)/shard_map/all_gather | solution.py:78
  517.9 2.9 convolution_bitcast_fusion.1
  520.8 0.0 all-reduce.7.cloned.1.call-start
  520.8 57.1 %all-gather.11.cloned.1.call-done = bf16[512,1152]{1,0:T(8,128)(2,1)} async-done(((bf16[32,1152]{1,0:T(8,128)(2,1)}), bf16[512,1152]{1,0:T(8,128)(2,1)}) %all-gather.11.cloned.1.call-update) | async-done | bytes 1179664 | tf_op jit(solution)/shard_map/all_gather | solution.py:79
  578.0 2.9 convolution_bitcast_fusion
  580.9 0.6 copy-done.15
  581.5 0.6 dynamic-slice
  582.1 0.6 dynamic-slice.2
  584.0 85.4 %psum.7 = f32[]{:T(128)} all-reduce(f32[]{:T(128)} %get-tuple-element.25), channel_id=1, replica_groups=mesh['img'=16,'txt'=16] {'img','txt'}, use_global_device_ids=true, to_apply=%region_5.6 | all-reduce | flops 1 | bytes 8 | tf_op jit(solution)/shard_map/psum | solution.py:72
  670.0 1.3 convolution_convert_fusion.1
  671.3 1.3 convolution_convert_fusion
  672.6 50.7 %all-reduce.5.cloned.1.call-done = f32[269,1152]{1,0:T(8,128)} async-done(((f32[269,1152]{1,0:T(8,128)}), f32[269,1152]{1,0:T(8,128)}) %all-reduce.5.cloned.1.call-update) | async-done | bytes 1239568
  723.2 1.0 constant_dynamic-slice_fusion.1
  724.3 0.8 copy.18
  725.1 156.3 %all-reduce.7.cloned.1.call-done = f32[269,1152]{1,0:T(8,128)} async-done(((f32[269,1152]{1,0:T(8,128)}), f32[269,1152]{1,0:T(8,128)}) %all-reduce.7.cloned.1.call-update) | async-done | bytes 1239568
  881.3 1.0 constant_dynamic-slice_fusion
  882.4 0.8 copy.19
  (43 shorter events, 0.3 us)
Async XLA Ops:
  7.2 1.1 copy-start
  7.2 87.1 %reduce-scatter.7.cloned.1.call-start = ((), (), s32[]{:S(2)}) async-start(), calls=%async_computation.4 | async-start | bytes 2506752 | tf_op jit(solution)/shard_map/reduce_scatter | solution.py:43
  11.5 1.0 copy-start.8
  11.5 1.2 copy-start.9
  11.5 151.5 %reduce-scatter.9.cloned.1.call-start = ((), (), s32[]{:S(2)}) async-start(), calls=%async_computation.6 | async-start | bytes 2506752 | tf_op jit(solution)/shard_map/reduce_scatter | solution.py:49
  14.9 79.4 %copy-start.11 = (bf16[32,1152]{1,0:T(8,128)(2,1)S(1)}, bf16[32,1152]{1,0:T(8,128)(2,1)}, u32[]{:S(2)}) copy-start(bf16[32,1152]{1,0:T(8,128)(2,1)} %param.9) | copy-start | bytes 221188
  14.9 148.1 %copy-start.12 = (bf16[32,1152]{1,0:T(8,128)(2,1)S(1)}, bf16[32,1152]{1,0:T(8,128)(2,1)}, u32[]{:S(2)}) copy-start(bf16[32,1152]{1,0:T(8,128)(2,1)} %param.12) | copy-start | bytes 221188
  14.9 213.1 %all-gather.5.cloned.1.call-start = ((), (), s32[]{:S(2)}) async-start(), calls=%async_computation.5 | async-start | bytes 1253376 | tf_op jit(solution)/shard_map/all_gather | solution.py:57
  96.0 192.1 %all-gather.7.cloned.1.call-start = ((), (), s32[]{:S(2)}) async-start(), calls=%async_computation.7 | async-start | bytes 1253376 | tf_op jit(solution)/shard_map/all_gather | solution.py:58
  164.7 125.0 %copy-start.13 = (s32[512]{0:T(512)S(1)}, s32[512]{0:T(512)}, u32[]{:S(2)}) copy-start(s32[512]{0:T(512)} %param.15) | copy-start | bytes 6148
  164.7 220.1 %reduce-scatter.11.cloned.1.call-start = ((), (), s32[]{:S(2)}) async-start(), calls=%async_computation.8 | async-start | bytes 2506752 | tf_op jit(solution)/shard_map/reduce_scatter | solution.py:74
  228.0 61.6 %copy-start.1 = (bf16[512,1152]{1,0:T(8,128)(2,1)S(1)}, bf16[512,1152]{1,0:T(8,128)(2,1)}, u32[]{:S(2)}) copy-start(bf16[512,1152]{1,0:T(8,128)(2,1)} %all-gather.5.cloned.1.call-done) | copy-start | bytes 3538948
  289.6 3.6 copy-start.2
  295.9 157.2 %reduce-scatter.13.cloned.1.call-start = ((), (), s32[]{:S(2)}) async-start(), calls=%async_computation.9 | async-start | bytes 2506752 | tf_op jit(solution)/shard_map/reduce_scatter | solution.py:75
  298.3 86.4 %copy-start.4 = (bf16[32,1152]{1,0:T(8,128)(2,1)S(1)}, bf16[32,1152]{1,0:T(8,128)(2,1)}, u32[]{:S(2)}) copy-start(bf16[32,1152]{1,0:T(8,128)(2,1)} %get-tuple-element.24) | copy-start | bytes 221188
  298.4 154.7 %copy-start.3 = (bf16[32,1152]{1,0:T(8,128)(2,1)S(1)}, bf16[32,1152]{1,0:T(8,128)(2,1)}, u32[]{:S(2)}) copy-start(bf16[32,1152]{1,0:T(8,128)(2,1)} %get-tuple-element.22) | copy-start | bytes 221188
  298.4 219.5 %copy-start.7 = (bf16[512,269]{0,1:T(8,128)(2,1)S(1)}, bf16[512,269]{0,1:T(8,128)(2,1)}, u32[]{:S(2)}) copy-start(bf16[512,269]{0,1:T(8,128)(2,1)} %param.10) | copy-start | bytes 826372
  298.4 219.5 %all-gather.9.cloned.1.call-start = ((), (), s32[]{:S(2)}) async-start(), calls=%async_computation.10 | async-start | bytes 1253376 | tf_op jit(solution)/shard_map/all_gather | solution.py:78
  387.6 190.4 %all-gather.11.cloned.1.call-start = ((), (), s32[]{:S(2)}) async-start(), calls=%async_computation.11 | async-start | bytes 1253376 | tf_op jit(solution)/shard_map/all_gather | solution.py:79
  455.9 267.4 %all-reduce.5.cloned.1.call-start = ((), (), s32[]{:S(2)}) async-start(), calls=%async_computation.12 | async-start | bytes 2506752
  520.8 360.5 %all-reduce.7.cloned.1.call-start = ((), (), s32[]{:S(2)}) async-start(), calls=%async_computation.13 | async-start | bytes 2506752
  580.8 0.7 copy-start.15
  580.8 1.3 copy-start.14
  580.8 89.2 %copy-start.5 = (bf16[512,1152]{1,0:T(8,128)(2,1)S(1)}, bf16[512,1152]{1,0:T(8,128)(2,1)}, u32[]{:S(2)}) copy-start(bf16[512,1152]{1,0:T(8,128)(2,1)} %all-gather.9.cloned.1.call-done) | copy-start | bytes 3538948
  580.9 90.4 %copy-start.6 = (bf16[512,1152]{1,0:T(8,128)(2,1)S(1)}, bf16[512,1152]{1,0:T(8,128)(2,1)}, u32[]{:S(2)}) copy-start(bf16[512,1152]{1,0:T(8,128)(2,1)} %all-gather.11.cloned.1.call-done) | copy-start | bytes 3538948
  670.0 1.3 copy-start.10
Sparse Core Ops, SparseCore 0:
  12.3 81.9 reduce-scatter.6
  97.0 65.9 reduce-scatter.8
  166.7 61.2 all-gather.4
  230.3 57.6 all-gather.6
  296.0 88.7 reduce-scatter.10
  387.2 65.8 reduce-scatter.12
  456.4 61.4 all-gather.8
  520.3 57.6 all-gather.10
  580.6 142.5 all-reduce.4
  725.7 155.5 all-reduce.6
where the time goes:
time: 892 us; the launch traced here: 891 us
  waiting for transfers between devices  745 us (84%)
  blocking collectives  85.4 us (10%)
  matrix products  22.4 us (3%)
  between operations  18.7 us (2%)
  other arithmetic  12.1 us (1%)
    unnamed x12, waiting for transfers between devices  207 us
    reduce_scatter x1, waiting for transfers between devices, on_device(): lax.psum_scatter(image_dir, 'txt', scatter_dimension=0, tiled=True)  86.3 us
    psum x1, blocking collectives, on_device(): total = lax.psum(partial_loss, ('img', 'txt'))  85.4 us
    reduce_scatter x1, waiting for transfers between devices, on_device(): lax.psum_scatter(jnp.dot(image_acts, image_proj, preferred_element_type=j...  79.3 us
    reduce_scatter x1, waiting for transfers between devices, on_device(): lax.psum_scatter(jnp.dot(text_acts, text_proj, preferred_element_type=jnp...  67 us
    reduce_scatter x1, waiting for transfers between devices, on_device(): text_up = lax.psum_scatter(text_dir, 'img', scatter_dimension=0, tiled=True)  65.5 us
    all_gather x1, waiting for transfers between devices, on_device(): image_back = lax.all_gather(image_grad, 'txt', axis=0, tiled=True)  62 us
    all_gather x1, waiting for transfers between devices, on_device(): image_block = lax.all_gather(image_embed, 'txt', axis=0, tiled=True)  61.9 us
  transfers between devices with their start and end apart: 10, of which 10 were waited for; matrix products, arithmetic and copies ran while one was open for 3% of the time, Pallas kernels for 0%

commit v1 on v0

--- a/solution.py
+++ b/solution.py
@@ -10,11 +10,6 @@
     return (values * inverse, inverse)
 
 
-def norm_backward(embed, upstream):
-    unit, inverse = normalize(embed)
-    return inverse * (upstream - unit * jnp.sum(unit * upstream, axis=-1, keepdims=True))
-
-
 def contract_rows(left, right):
     return lax.dot_general(
         left, right, (((0,), (0,)), ((), ())), preferred_element_type=jnp.float32
@@ -25,6 +20,23 @@
     return lax.dot_general(
         left, right, (((1,), (1,)), ((), ())), preferred_element_type=jnp.float32
     )
+
+
+def scatter_sum(parts, axis):
+    count = lax.axis_size(axis)
+    blocks = parts.astype(jnp.bfloat16).reshape((count, -1) + parts.shape[1:])
+    return jnp.sum(lax.all_to_all(blocks, axis, 0, 0).astype(jnp.float32), axis=0)
+
+
+def gather(block, axis):
+    count = lax.axis_size(axis)
+    copies = jnp.broadcast_to(block[None], (count,) + block.shape)
+    return lax.all_to_all(copies, axis, 0, 0).reshape((-1,) + block.shape[1:])
+
+
+def project(embed, upstream):
+    unit, inverse = normalize(embed)
+    return inverse * (upstream - unit * jnp.sum(unit * upstream, axis=-1, keepdims=True))
 
 
 def on_device(
@@ -40,22 +52,16 @@
 ):
     rows = image_hidden.shape[0]
     total_rows = rows * lax.axis_size("img") * lax.axis_size("txt")
-    image_sum = lax.psum_scatter(
-        jnp.dot(image_acts, image_proj, preferred_element_type=jnp.float32),
-        "txt",
-        scatter_dimension=0,
-        tiled=True,
+    image_sum = scatter_sum(
+        jnp.dot(image_acts, image_proj, preferred_element_type=jnp.float32), "txt"
     )
-    text_sum = lax.psum_scatter(
-        jnp.dot(text_acts, text_proj, preferred_element_type=jnp.float32),
-        "img",
-        scatter_dimension=0,
-        tiled=True,
+    text_sum = scatter_sum(
+        jnp.dot(text_acts, text_proj, preferred_element_type=jnp.float32), "img"
     )
     image_embed = (image_hidden.astype(jnp.float32) + image_sum).astype(jnp.bfloat16)
     text_embed = (text_hidden.astype(jnp.float32) + text_sum).astype(jnp.bfloat16)
-    image_block = lax.all_gather(image_embed, "txt", axis=0, tiled=True)
-    text_block = lax.all_gather(text_embed, "img", axis=0, tiled=True)
+    image_block = gather(image_embed, "txt")
+    text_block = gather(text_embed, "img")
     image_unit = normalize(image_block)[0].astype(jnp.bfloat16)
     text_unit = normalize(text_block)[0].astype(jnp.bfloat16)
     scale = jnp.exp(log_scale[0])
@@ -71,20 +77,14 @@
     text_dir = scale * contract_rows(slope, image_unit)
     total = lax.psum(partial_loss, ("img", "txt"))
     loss = jnp.reshape(total / total_rows, (1,))
-    image_up = lax.psum_scatter(image_dir, "txt", scatter_dimension=0, tiled=True)
-    text_up = lax.psum_scatter(text_dir, "img", scatter_dimension=0, tiled=True)
-    image_grad = norm_backward(image_embed, image_up).astype(jnp.bfloat16)
-    text_grad = norm_backward(text_embed, text_up).astype(jnp.bfloat16)
-    image_back = lax.all_gather(image_grad, "txt", axis=0, tiled=True)
-    text_back = lax.all_gather(text_grad, "img", axis=0, tiled=True)
+    image_grad = scatter_sum(project(image_block, image_dir), "txt").astype(jnp.bfloat16)
+    text_grad = scatter_sum(project(text_block, text_dir), "img").astype(jnp.bfloat16)
+    image_back = gather(image_grad, "txt")
+    text_back = gather(text_grad, "img")
     image_act_grad = contract_cols(image_back, image_proj).astype(jnp.bfloat16)
     text_act_grad = contract_cols(text_back, text_proj).astype(jnp.bfloat16)
-    image_proj_grad = lax.psum_scatter(
-        contract_rows(image_acts, image_back), "img", scatter_dimension=1, tiled=True
-    )
-    text_proj_grad = lax.psum_scatter(
-        contract_rows(text_acts, text_back), "txt", scatter_dimension=1, tiled=True
-    )
+    image_proj_grad = scatter_sum(contract_rows(image_back, image_acts), "img").T
+    text_proj_grad = scatter_sum(contract_rows(text_back, text_acts), "txt").T
     return (
         loss,
         image_grad,

time: 892 us -> 368 us (0.41)
  waiting for transfers between devices: 745 us -> 165 us
  starting transfers between devices: 0.42 us -> 56.4 us
  blocking collectives: 85.4 us -> 104 us
  between operations: 18.7 us -> 3.94 us
    reduce_scatter x4 -> x0, waiting for transfers between devices: 298 us -> none  [the longest x1 86.3 us: on_device(): lax.psum_scatter(image_dir, 'txt', scatter_dimension=0, tiled=True)]
    all_gather x4 -> x0, waiting for transfers between devices: 239 us -> none  [the longest x1 62 us: on_device(): image_back = lax.all_gather(image_grad, 'txt', axis=0, tiled=True)]
    unnamed x12 -> x0, waiting for transfers between devices: 207 us -> none
    all_to_all x0 -> x9, waiting for transfers between devices: none -> 165 us  [the longest x4 83.5 us: gather(): return lax.all_to_all(copies, axis, 0, 0).reshape((-1,) + block.shape[1:])]
    all_to_all x0 -> x9, starting transfers between devices: none -> 56.4 us  [the longest x5 32.1 us: scatter_sum(): lax.all_to_all(blocks, axis, 0, 0).astype(jnp.float32)]
    all_to_all x0 -> x1, blocking collectives: none -> 26.2 us  [scatter_sum(): lax.all_to_all(blocks, axis, 0, 0).astype(jnp.float32)]
  transfers between devices with their start and end apart: 10 -> 9, of which waited for: 10 -> 8; matrix products, arithmetic and copies ran while one was open for 3% -> 5% of each run, Pallas kernels for 0% -> 0%
where the time goes in v1:
time: 368 us; the launch traced here: 367 us
  waiting for transfers between devices  165 us (45%)
  blocking collectives  104 us (28%)
  starting transfers between devices  56.4 us (15%)
  matrix products  14.6 us (4%)
  local copies, waits for them, and re-layouts  12.8 us (3%)
  other arithmetic  10.2 us (3%)
  between operations  3.94 us (1%)
    all_to_all x4, waiting for transfers between devices, gather(): return lax.all_to_all(copies, axis, 0, 0).reshape((-1,) + block.shape[1:])  83.5 us
    all_to_all x5, waiting for transfers between devices, scatter_sum(): lax.all_to_all(blocks, axis, 0, 0).astype(jnp.float32)  81.9 us
    psum x1, blocking collectives, on_device(): total = lax.psum(partial_loss, ('img', 'txt'))  77.5 us
    all_to_all x5, starting transfers between devices, scatter_sum(): lax.all_to_all(blocks, axis, 0, 0).astype(jnp.float32)  32.1 us
    all_to_all x1, blocking collectives, scatter_sum(): lax.all_to_all(blocks, axis, 0, 0).astype(jnp.float32)  26.2 us
    all_to_all x4, starting transfers between devices, gather(): return lax.all_to_all(copies, axis, 0, 0).reshape((-1,) + block.shape[1:])  24.3 us
  transfers between devices with their start and end apart: 9, of which 8 were waited for; matrix products, arithmetic and copies ran while one was open for 5% of the time, Pallas kernels for 0%

profile of v1, /device:TPU:1, one launch (start us, length us, event | category | flops | bytes accessed | tf_op | source)
XLA Modules:
  0.0 367.0 jit_solution(7379855974241862776)
XLA Ops:
  0.6 1.1 copy-done
  1.7 2.8 convolution_convert_fusion.1
  4.5 8.6 %all-to-all-start = ((bf16[16,32,1152]{2,1,0:T(8,128)(2,1)}), bf16[16,32,1152]{2,1,0:T(8,128)(2,1)S(1)}, u32[]{:S(2)}, u32[]{:S(2)}) async-start(bf16[16,32,1152]{2,1,0:T(8,128)(2,1)} %bitcast.1), calls=%async_computation | async-start | bytes 2359296 | tf_op jit(solution)/shard_map/all_to_all | solution.py:28
  13.1 1.9 convolution_convert_fusion
  15.0 16.7 %all-to-all-done = bf16[16,32,1152]{2,1,0:T(8,128)(2,1)S(1)} async-done(((bf16[16,32,1152]{2,1,0:T(8,128)(2,1)}), bf16[16,32,1152]{2,1,0:T(8,128)(2,1)S(1)}, u32[]{:S(2)}, u32[]{:S(2)}) %all-to-all-start) | async-done | bytes 1179680 | tf_op jit(solution)/shard_map/all_to_all | solution.py:28
  31.8 8.3 %all-to-all-start.2 = ((bf16[16,32,1152]{2,1,0:T(8,128)(2,1)}), bf16[16,32,1152]{2,1,0:T(8,128)(2,1)S(1)}, u32[]{:S(2)}, u32[]{:S(2)}) async-start(bf16[16,32,1152]{2,1,0:T(8,128)(2,1)} %bitcast.56), calls=%async_computation.2 | async-start | bytes 2359296 | tf_op jit(solution)/shard_map/all_to_all | solution.py:28
  40.3 0.7 copy-done.8
  41.0 26.4 %all-to-all-done.2 = bf16[16,32,1152]{2,1,0:T(8,128)(2,1)S(1)} async-done(((bf16[16,32,1152]{2,1,0:T(8,128)(2,1)}), bf16[16,32,1152]{2,1,0:T(8,128)(2,1)S(1)}, u32[]{:S(2)}, u32[]{:S(2)}) %all-to-all-start.2) | async-done | bytes 1179680 | tf_op jit(solution)/shard_map/all_to_all | solution.py:28
  67.3 1.1 broadcast_in_dim.8
  68.4 8.7 %all-to-all-start.1 = ((bf16[16,32,1152]{2,1,0:T(8,128)(2,1)}), bf16[16,32,1152]{2,1,0:T(8,128)(2,1)S(1)}, u32[]{:S(2)}, u32[]{:S(2)}) async-start(bf16[16,32,1152]{2,1,0:T(8,128)(2,1)} %broadcast_in_dim.8), calls=%async_computation.1 | async-start | bytes 2359296 | tf_op jit(solution)/shard_map/all_to_all | solution.py:34
  77.4 0.7 copy-done.9
  78.1 17.7 %all-to-all-done.1 = bf16[16,32,1152]{2,1,0:T(8,128)(2,1)S(1)} async-done(((bf16[16,32,1152]{2,1,0:T(8,128)(2,1)}), bf16[16,32,1152]{2,1,0:T(8,128)(2,1)S(1)}, u32[]{:S(2)}, u32[]{:S(2)}) %all-to-all-start.1) | async-done | bytes 1179680 | tf_op jit(solution)/shard_map/all_to_all | solution.py:34
  95.8 1.1 broadcast_in_dim.9
  97.0 3.7 %all-to-all-start.3 = ((bf16[16,32,1152]{2,1,0:T(8,128)(2,1)}), bf16[16,32,1152]{2,1,0:T(8,128)(2,1)S(1)}, u32[]{:S(2)}, u32[]{:S(2)}) async-start(bf16[16,32,1152]{2,1,0:T(8,128)(2,1)} %broadcast_in_dim.9), calls=%async_computation.3 | async-start | bytes 2359296 | tf_op jit(solution)/shard_map/all_to_all | solution.py:34
  102.0 0.3 multiply_reduce_fusion.3
  102.4 1.3 fusion.1
  103.7 1.3 multiply_convert_fusion.3
  105.0 23.3 %all-to-all-done.3 = bf16[16,32,1152]{2,1,0:T(8,128)(2,1)S(1)} async-done(((bf16[16,32,1152]{2,1,0:T(8,128)(2,1)}), bf16[16,32,1152]{2,1,0:T(8,128)(2,1)S(1)}, u32[]{:S(2)}, u32[]{:S(2)}) %all-to-all-start.3) | async-done | bytes 1179680 | tf_op jit(solution)/shard_map/all_to_all | solution.py:34
  128.3 0.3 multiply_reduce_fusion.2
  128.7 0.3 multiply_convert_fusion.2
  128.9 1.0 copy-done.1
  129.9 2.2 fusion.7
  132.1 1.2 multiply_reduce_fusion
  133.3 1.6 multiply_convert_fusion
  134.9 1.2 multiply_reduce_fusion.1
  136.1 0.5 multiply_convert_fusion.1
  136.6 26.2 %all_to_all.50 = bf16[16,32,1152]{2,1,0:T(8,128)(2,1)S(1)} all-to-all(bf16[16,32,1152]{2,1,0:T(8,128)(2,1)S(1)} %bitcast.52), channel_id=1, replica_groups=mesh['img'=16,'txt'=16] {'txt'}, dimensions={0} | all-to-all | bytes 2359296 | tf_op jit(solution)/shard_map/all_to_all | solution.py:28
  162.8 3.7 %all-to-all-start.5 = ((bf16[16,32,1152]{2,1,0:T(8,128)(2,1)}), bf16[16,32,1152]{2,1,0:T(8,128)(2,1)S(1)}, u32[]{:S(2)}, u32[]{:S(2)}) async-start(bf16[16,32,1152]{2,1,0:T(8,128)(2,1)} %bitcast.10), calls=%async_computation.5 | async-start | bytes 2359296 | tf_op jit(solution)/shard_map/all_to_all | solution.py:28
  166.6 0.2 reduce_sum.119
  166.7 27.7 %all-to-all-done.5 = bf16[16,32,1152]{2,1,0:T(8,128)(2,1)S(1)} async-done(((bf16[16,32,1152]{2,1,0:T(8,128)(2,1)}), bf16[16,32,1152]{2,1,0:T(8,128)(2,1)S(1)}, u32[]{:S(2)}, u32[]{:S(2)}) %all-to-all-start.5) | async-done | bytes 1179680 | tf_op jit(solution)/shard_map/all_to_all | solution.py:28
  194.4 1.1 broadcast_in_dim.10
  195.5 8.0 %all-to-all-start.6 = ((bf16[16,32,1152]{2,1,0:T(8,128)(2,1)}), bf16[16,32,1152]{2,1,0:T(8,128)(2,1)S(1)}, u32[]{:S(2)}, u32[]{:S(2)}) async-start(bf16[16,32,1152]{2,1,0:T(8,128)(2,1)} %broadcast_in_dim.10), calls=%async_computation.6 | async-start | bytes 2359296 | tf_op jit(solution)/shard_map/all_to_all | solution.py:34
  203.8 18.5 %all-to-all-done.6 = bf16[16,32,1152]{2,1,0:T(8,128)(2,1)S(1)} async-done(((bf16[16,32,1152]{2,1,0:T(8,128)(2,1)}), bf16[16,32,1152]{2,1,0:T(8,128)(2,1)S(1)}, u32[]{:S(2)}, u32[]{:S(2)}) %all-to-all-start.6) | async-done | bytes 1179680 | tf_op jit(solution)/shard_map/all_to_all | solution.py:34
  222.3 1.2 broadcast_in_dim.11
  223.5 3.8 %all-to-all-start.7 = ((bf16[16,32,1152]{2,1,0:T(8,128)(2,1)}), bf16[16,32,1152]{2,1,0:T(8,128)(2,1)S(1)}, u32[]{:S(2)}, u32[]{:S(2)}) async-start(bf16[16,32,1152]{2,1,0:T(8,128)(2,1)} %broadcast_in_dim.11), calls=%async_computation.7 | async-start | bytes 2359296 | tf_op jit(solution)/shard_map/all_to_all | solution.py:34
  227.3 1.4 convolution_convert_fusion.3
  228.7 2.3 copy.16
  231.0 23.9 %all-to-all-done.7 = bf16[16,32,1152]{2,1,0:T(8,128)(2,1)S(1)} async-done(((bf16[16,32,1152]{2,1,0:T(8,128)(2,1)}), bf16[16,32,1152]{2,1,0:T(8,128)(2,1)S(1)}, u32[]{:S(2)}, u32[]{:S(2)}) %all-to-all-start.7) | async-done | bytes 1179680 | tf_op jit(solution)/shard_map/all_to_all | solution.py:34
  254.9 6.8 %all-to-all-start.8 = ((bf16[16,72,269]{2,1,0:T(8,128)(2,1)}), bf16[16,72,269]{2,1,0:T(8,128)(2,1)}, u32[]{:S(2)}, u32[]{:S(2)}) async-start(bf16[16,72,269]{2,1,0:T(8,128)(2,1)} %bitcast.53), calls=%async_computation.8 | async-start | bytes 1769472 | tf_op jit(solution)/shard_map/all_to_all | solution.py:28
  261.7 77.5 %psum.7 = f32[]{:T(128)} all-reduce(f32[]{:T(128)} %get-tuple-element.9), channel_id=1, replica_groups=mesh['img'=16,'txt'=16] {'img','txt'}, use_global_device_ids=true, to_apply=%region_5.6 | all-reduce | flops 1 | bytes 8 | tf_op jit(solution)/shard_map/psum | solution.py:78
  339.9 1.4 convolution_convert_fusion.2
  341.3 2.3 copy.17
  343.6 4.7 %all-to-all-start.9 = ((bf16[16,72,269]{2,1,0:T(8,128)(2,1)}), bf16[16,72,269]{2,1,0:T(8,128)(2,1)}, u32[]{:S(2)}, u32[]{:S(2)}) async-start(bf16[16,72,269]{2,1,0:T(8,128)(2,1)} %bitcast.54), calls=%async_computation.9 | async-start | bytes 1769472 | tf_op jit(solution)/shard_map/all_to_all | solution.py:28
  348.3 1.3 convolution_convert_fusion.5
  349.6 2.0 convert_reduce_fusion.3
  351.5 1.3 convolution_convert_fusion.4
  352.8 11.1 %all-to-all-done.9 = bf16[16,72,269]{2,1,0:T(8,128)(2,1)} async-done(((bf16[16,72,269]{2,1,0:T(8,128)(2,1)}), bf16[16,72,269]{2,1,0:T(8,128)(2,1)}, u32[]{:S(2)}, u32[]{:S(2)}) %all-to-all-start.9) | async-done | bytes 619808 | tf_op jit(solution)/shard_map/all_to_all | solution.py:28
  363.9 2.0 convert_reduce_fusion.2
  (33 shorter events, 0.8 us)
Async XLA Ops:
  0.6 1.1 copy-start
  4.5 8.6 %copy-start.6 = (bf16[512,269]{0,1:T(8,128)(2,1)S(1)}, bf16[512,269]{0,1:T(8,128)(2,1)}, u32[]{:S(2)}) copy-start(bf16[512,269]{0,1:T(8,128)(2,1)} %param.13) | copy-start | bytes 826372
  4.5 8.6 %copy-start.10 = (bf16[269,1152]{1,0:T(8,128)(2,1)S(1)}, bf16[269,1152]{1,0:T(8,128)(2,1)}, u32[]{:S(2)}) copy-start(bf16[269,1152]{1,0:T(8,128)(2,1)} %param.14) | copy-start | bytes 1859332
  4.5 27.2 %all-to-all-start = ((bf16[16,32,1152]{2,1,0:T(8,128)(2,1)}), bf16[16,32,1152]{2,1,0:T(8,128)(2,1)S(1)}, u32[]{:S(2)}, u32[]{:S(2)}) async-start(bf16[16,32,1152]{2,1,0:T(8,128)(2,1)} %bitcast.1), calls=%async_computation | async-start | bytes 2359296 | tf_op jit(solution)/shard_map/all_to_all | solution.py:28
  31.8 35.6 %all-to-all-start.2 = ((bf16[16,32,1152]{2,1,0:T(8,128)(2,1)}), bf16[16,32,1152]{2,1,0:T(8,128)(2,1)S(1)}, u32[]{:S(2)}, u32[]{:S(2)}) async-start(bf16[16,32,1152]{2,1,0:T(8,128)(2,1)} %bitcast.56), calls=%async_computation.2 | async-start | bytes 2359296 | tf_op jit(solution)/shard_map/all_to_all | solution.py:28
  40.1 0.9 copy-start.8
  68.4 27.4 %all-to-all-start.1 = ((bf16[16,32,1152]{2,1,0:T(8,128)(2,1)}), bf16[16,32,1152]{2,1,0:T(8,128)(2,1)S(1)}, u32[]{:S(2)}, u32[]{:S(2)}) async-start(bf16[16,32,1152]{2,1,0:T(8,128)(2,1)} %broadcast_in_dim.8), calls=%async_computation.1 | async-start | bytes 2359296 | tf_op jit(solution)/shard_map/all_to_all | solution.py:34
  77.2 0.9 copy-start.9
  97.0 31.3 %all-to-all-start.3 = ((bf16[16,32,1152]{2,1,0:T(8,128)(2,1)}), bf16[16,32,1152]{2,1,0:T(8,128)(2,1)S(1)}, u32[]{:S(2)}, u32[]{:S(2)}) async-start(bf16[16,32,1152]{2,1,0:T(8,128)(2,1)} %broadcast_in_dim.9), calls=%async_computation.3 | async-start | bytes 2359296 | tf_op jit(solution)/shard_map/all_to_all | solution.py:34
  128.7 1.3 copy-start.1
  128.7 1.3 copy-start.12
  129.9 2.2 copy-start.2
  162.8 31.6 %all-to-all-start.5 = ((bf16[16,32,1152]{2,1,0:T(8,128)(2,1)}), bf16[16,32,1152]{2,1,0:T(8,128)(2,1)S(1)}, u32[]{:S(2)}, u32[]{:S(2)}) async-start(bf16[16,32,1152]{2,1,0:T(8,128)(2,1)} %bitcast.10), calls=%async_computation.5 | async-start | bytes 2359296 | tf_op jit(solution)/shard_map/all_to_all | solution.py:28
  166.7 28.8 %copy-start.3 = (bf16[32,1152]{1,0:T(8,128)(2,1)}, bf16[32,1152]{1,0:T(8,128)(2,1)S(1)}, u32[]{:S(2)}) copy-start(bf16[32,1152]{1,0:T(8,128)(2,1)S(1)} %reduce_sum.119) | copy-start | bytes 221188
  195.5 26.8 %all-to-all-start.6 = ((bf16[16,32,1152]{2,1,0:T(8,128)(2,1)}), bf16[16,32,1152]{2,1,0:T(8,128)(2,1)S(1)}, u32[]{:S(2)}, u32[]{:S(2)}) async-start(bf16[16,32,1152]{2,1,0:T(8,128)(2,1)} %broadcast_in_dim.10), calls=%async_computation.6 | async-start | bytes 2359296 | tf_op jit(solution)/shard_map/all_to_all | solution.py:34
  203.8 19.7 %copy-start.4 = (bf16[32,1152]{1,0:T(8,128)(2,1)}, bf16[32,1152]{1,0:T(8,128)(2,1)S(1)}, u32[]{:S(2)}) copy-start(bf16[32,1152]{1,0:T(8,128)(2,1)S(1)} %reduce_sum.121) | copy-start | bytes 221188
  223.5 3.8 %copy-start.5 = (bf16[512,269]{0,1:T(8,128)(2,1)S(1)}, bf16[512,269]{0,1:T(8,128)(2,1)}, u32[]{:S(2)}) copy-start(bf16[512,269]{0,1:T(8,128)(2,1)} %param.10) | copy-start | bytes 826372
  223.5 31.4 %all-to-all-start.7 = ((bf16[16,32,1152]{2,1,0:T(8,128)(2,1)}), bf16[16,32,1152]{2,1,0:T(8,128)(2,1)S(1)}, u32[]{:S(2)}, u32[]{:S(2)}) async-start(bf16[16,32,1152]{2,1,0:T(8,128)(2,1)} %broadcast_in_dim.11), calls=%async_computation.7 | async-start | bytes 2359296 | tf_op jit(solution)/shard_map/all_to_all | solution.py:34
  231.0 108.9 %copy-start.7 = (bf16[512,269]{0,1:T(8,128)(2,1)S(1)}, bf16[512,269]{0,1:T(8,128)(2,1)}, u32[]{:S(2)}) copy-start(bf16[512,269]{0,1:T(8,128)(2,1)} %param.13) | copy-start | bytes 826372
  254.9 88.7 %all-to-all-start.8 = ((bf16[16,72,269]{2,1,0:T(8,128)(2,1)}), bf16[16,72,269]{2,1,0:T(8,128)(2,1)}, u32[]{:S(2)}, u32[]{:S(2)}) async-start(bf16[16,72,269]{2,1,0:T(8,128)(2,1)} %bitcast.53), calls=%async_computation.8 | async-start | bytes 1769472 | tf_op jit(solution)/shard_map/all_to_all | solution.py:28
  343.6 20.3 %all-to-all-start.9 = ((bf16[16,72,269]{2,1,0:T(8,128)(2,1)}), bf16[16,72,269]{2,1,0:T(8,128)(2,1)}, u32[]{:S(2)}, u32[]{:S(2)}) async-start(bf16[16,72,269]{2,1,0:T(8,128)(2,1)} %bitcast.54), calls=%async_computation.9 | async-start | bytes 1769472 | tf_op jit(solution)/shard_map/all_to_all | solution.py:28
  348.3 3.2 copy-start.11
